TPU v7x, 32 devices: a whole 2x2x4 slice. The times are simulated.
32 devices in a mesh: dom: 8 (over z, y), lev: 4 (over x, core).
Axes of the slice: x: 2, y: 2, z: 4, core: 2. Of those that a mesh axis runs over, the one named last changes fastest.
Arguments:
- source: bfloat16 [8, 128, 16384], P(None, 'lev', 'dom'), may hold values from -6 to 6
- send_slots: int32 [8, 5, 4], P('dom'), may hold values from 0 to 15
- intersection_col: int32 [8, 32768], P(None, 'dom'), may hold values from 0 to 2559, as said below
- intersection_wt: float32 [8, 32768], P(None, 'dom'), may hold values from 0.05 to 1
- intersection_count: int32 [32768], P('dom'), may hold values from 1 to 8
- neighbours: int32 [6, 32768], P(None, 'dom'), may hold values from 0 to 4351, as said below
- land_mask: int32 [32768], P('dom'), may hold values 0 or 1
- diffusivity: float32 [8, 128], P(None, 'lev'), may hold values from 0.02 to 0.15
Outputs:
- updated: float32 [8, 128, 32768], P(None, 'lev', 'dom')
Inputs may be any that keep to these rules, and one draw needn't show every extreme that they name: `intersection_col`: entries name columns of the target domain's received set; the 8 entries of one target cell name different columns. `neighbours`: a neighbour lies within 128 cells of its cell in the cyclic global cell order; the entry is its position among the domain's cells preceded and followed by 128 cells of the adjacent domains.
All inputs are finite; a program needn't handle non-finite values. No bound on the sum of `land_mask` on one device may be relied on, other than what follows from the above.
Results may differ from a plain program's by a relative error of at most 0.0024.
Values may be sent and summed in bfloat16 or wider, within the bound.
A program may use at most 64 MiB of HBM per device.

v0:
```python
import jax
import jax.numpy as jnp
from jax import lax
from jax.sharding import PartitionSpec as P

B = 128
CAP = 4
R = 2
K = 8
NN = 6
H = 128


vertical_rate = 0.1


def passed_along(value, axis, steps):
    count = lax.axis_size(axis)
    pairs = [(source, (source + steps) % count) for source in range(count)]
    return lax.ppermute(value, axis, pairs)


def extended(block, sides, width, periodic):
    for axis, dim in sides:
        count = lax.axis_size(axis)
        forward = [(i, i + 1) for i in range(count - 1)]
        if periodic:
            forward.append((count - 1, 0))
        backward = [(target, source) for source, target in forward]
        low = lax.ppermute(
            lax.slice_in_dim(block, block.shape[dim] - width, None, axis=dim), axis, forward
        )
        high = lax.ppermute(lax.slice_in_dim(block, 0, width, axis=dim), axis, backward)
        block = jnp.concatenate([low, block, high], axis=dim)
    return block


def on_device(
    source,
    send_slots,
    intersection_col,
    intersection_wt,
    intersection_count,
    neighbours,
    land_mask,
    diffusivity,
):
    fields, levels, columns = source.shape
    stacked = fields * levels
    per_domain = columns // B
    targets = land_mask.shape[0]
    blockset = CAP * B
    block_ids = lax.broadcasted_iota(jnp.int32, (2 * R + 1, CAP, per_domain), 2)
    picker = (send_slots[0][:, :, None] == block_ids).astype(jnp.bfloat16)
    table = jnp.einsum(
        "ocp,spb->oscb",
        picker,
        source.reshape(stacked, per_domain, B),
        preferred_element_type=jnp.float32,
    )
    outgoing = table.astype(jnp.bfloat16).reshape(2 * R + 1, stacked, blockset)
    arrived = [outgoing[R] for offset in range(2 * R + 1)]
    for offset in range(2 * R + 1):
        if offset != R:
            arrived[offset] = passed_along(outgoing[offset], "dom", offset - R)
    received = jnp.stack(arrived, axis=1).reshape(stacked, (2 * R + 1) * blockset)
    width = received.shape[1]
    slot_index = lax.broadcasted_iota(jnp.int32, (K, targets), 0)
    live_wt = jnp.where(slot_index < intersection_count[None, :], intersection_wt, 0.0)
    shares = (live_wt / jnp.sum(live_wt, axis=0, keepdims=True)).astype(jnp.bfloat16)
    tile = min(512, targets)
    count_blocks = targets // tile
    tiled_cols = jnp.transpose(intersection_col.reshape(K, count_blocks, tile), (1, 0, 2))
    tiled_shares = jnp.transpose(shares.reshape(K, count_blocks, tile), (1, 0, 2))

    def remap_block(inputs):
        block_cols, block_shares = inputs
        column_ids = lax.broadcasted_iota(jnp.int32, (tile, width), 1)
        dense = jnp.zeros((tile, width), jnp.bfloat16)
        for slot in range(K):
            dense = jnp.where(
                block_cols[slot][:, None] == column_ids, block_shares[slot][:, None], dense
            )
        return jnp.einsum("fc,tc->ft", received, dense, preferred_element_type=jnp.float32)

    remapped_blocks = lax.map(remap_block, (tiled_cols, tiled_shares))
    remapped = jnp.moveaxis(remapped_blocks, 0, 1).reshape(fields, levels, targets)
    ocean = land_mask.astype(jnp.float32)
    extended_field, extended_ocean = (
        extended(remapped, (("dom", 2),), H, True),
        extended(ocean.reshape(1, 1, targets), (("dom", 2),), H, True),
    )
    ocean_flat = extended_ocean[0, 0]
    field_flat = extended_field.reshape(stacked, targets + 2 * H)
    remapped_flat = remapped.reshape(stacked, targets)
    window = tile + 2 * H
    tiled_near = jnp.transpose(neighbours.reshape(NN, count_blocks, tile), (1, 0, 2))

    def stencil_block(inputs):
        block_index, near = inputs
        start = block_index * tile
        field_window = lax.dynamic_slice_in_dim(field_flat, start, window, 1)
        ocean_window = lax.dynamic_slice_in_dim(ocean_flat, start, window, 0)
        own = lax.dynamic_slice_in_dim(remapped_flat, start, tile, 1)
        window_ids = lax.broadcasted_iota(jnp.int32, (tile, window), 1)
        weights = jnp.zeros((tile, window), jnp.float32)
        for neighbour in range(NN):
            local_pos = near[neighbour] - start
            weights = weights + jnp.where(
                local_pos[:, None] == window_ids, ocean_window[None, :], 0.0
            )
        gathered = jnp.einsum(
            "rc,tc->rt",
            field_window,
            weights,
            precision=lax.Precision.HIGHEST,
            preferred_element_type=jnp.float32,
        )
        return gathered - jnp.sum(weights, axis=1)[None, :] * own

    lateral_blocks = lax.map(stencil_block, (jnp.arange(count_blocks, dtype=jnp.int32), tiled_near))
    lateral = jnp.moveaxis(lateral_blocks, 0, 1).reshape(fields, levels, targets)
    stacked_levels = extended(remapped.astype(jnp.bfloat16), (("lev", 1),), 1, False).astype(
        remapped.dtype
    )
    vertical = stacked_levels[:, 2:, :] + stacked_levels[:, :-2, :] - 2.0 * remapped
    return ocean[None, None, :] * (
        remapped + diffusivity[:, :, None] * lateral + vertical_rate * vertical
    )


def solution(mesh):
    return jax.shard_map(
        on_device,
        mesh=mesh,
        in_specs=(
            P(None, "lev", "dom"),
            P("dom", None, None),
            P(None, "dom"),
            P(None, "dom"),
            P("dom"),
            P(None, "dom"),
            P("dom"),
            P(None, "lev"),
        ),
        out_specs=P(None, "lev", "dom"),
        check_vma=False,
    )
```

profile of v0, /device:TPU:1, one launch (start us, length us, event | category | flops | bytes accessed | tf_op | source)
XLA Modules:
  0.0 215.4 jit_solution(17963043451618907612)
XLA Ops:
  5.9 4.1 %collective-permute-start = (bf16[256,512]{0,1:T(8,128)(2,1)}, bf16[256,512]{0,1:T(8,128)(2,1)S(1)}, u32[]{:S(2)}, u32[]{:S(2)}) collective-permute-start(bf16[256,512]{0,1:T(8,128)(2,1)} %bitcast.26), channel_id=1, source_target_pairs={{0,24},{4,28},{8,0},{12,4},{16,8},{20,12},{24,16},{28,20},{1,25},{... | collective-permute-start | bytes 786440 | tf_op jit(solution)/shard_map/ppermute | solution.py:20
  17.6 5.5 %collective-permute-done.6 = f32[1,1,128]{2,1,0:T(1,128)S(1)} collective-permute-done((f32[1,1,128]{2,1,0:T(1,128)S(1)}, f32[1,1,128]{2,1,0:T(1,128)S(1)}, u32[]{:S(2)}, u32[]{:S(2)}) %collective-permute-start.6) | collective-permute-done | bytes 544 | tf_op jit(solution)/shard_map/ppermute | solution.py:30
  26.8 5.6 %collective-permute-done.3 = bf16[256,512]{0,1:T(8,128)(2,1)S(1)} collective-permute-done((bf16[256,512]{0,1:T(8,128)(2,1)S(1)}, bf16[256,512]{0,1:T(8,128)(2,1)S(1)}, u32[]{:S(2)}, u32[]{:S(2)}) %collective-permute-start.3) | collective-permute-done | bytes 262176 | tf_op jit(solution)/shard_map/ppermute | solution.py:20
  34.0 52.6 %while.20 = (s32[]{:T(128)}, f32[8,256,512]{1,2,0:T(8,128)}, s32[8,8,512]{2,1,0:T(8,128)}, bf16[8,8,512]{2,1,0:T(8,128)(2,1)S(1)}, bf16[256,2560]{1,0:T(8,128)(2...) while((s32[]{:T(128)}, f32[8,256,512]{1,2,0:T(8,128)}, ...), condition=%wide.region_2.3_spmd, body=%wide.region_1.2_spmd.sunk | while | flops 692060160 | bytes 1909529 | solution.py:86
  35.1 5.5 %fusion.72 = f32[8,256,512]{1,2,0:T(8,128)} fusion(f32[8,256,512]{1,2,0:T(8,128)} %get-tuple-element.276, s32[]{:T(128)} %get-tuple-element.275, bf16[256,2560]{1,0:T(8,128)(2,1)S(1)} %get-tuple-element.293, s32[512]{0:T(512)S(1)} %bitcast.128, s32[512]{0:T(512)S(1)} %bitcast.122, s32[512]{0:T(512)S(1)} %bitcast.123, s32[512]{0:T(512)S(1)} %bitcast.124, ...), kind=kOutput, calls=%fused_computation.53.clone.1 | convolution fusion | flops 692060160 | bytes 1860096 | tf_op jit(solution)/shard_map/while/body/eval_jaxpr/fc,tc->ft/dot_general | solution.py:84
  41.7 5.5 %fusion.72 = f32[8,256,512]{1,2,0:T(8,128)} fusion(f32[8,256,512]{1,2,0:T(8,128)} %get-tuple-element.276, s32[]{:T(128)} %get-tuple-element.275, bf16[256,2560]{1,0:T(8,128)(2,1)S(1)} %get-tuple-element.293, s32[512]{0:T(512)S(1)} %bitcast.128, s32[512]{0:T(512)S(1)} %bitcast.122, s32[512]{0:T(512)S(1)} %bitcast.123, s32[512]{0:T(512)S(1)} %bitcast.124, ...), kind=kOutput, calls=%fused_computation.53.clone.1 | convolution fusion | flops 692060160 | bytes 1860096 | tf_op jit(solution)/shard_map/while/body/eval_jaxpr/fc,tc->ft/dot_general | solution.py:84
  48.3 5.5 %fusion.72 = f32[8,256,512]{1,2,0:T(8,128)} fusion(f32[8,256,512]{1,2,0:T(8,128)} %get-tuple-element.276, s32[]{:T(128)} %get-tuple-element.275, bf16[256,2560]{1,0:T(8,128)(2,1)S(1)} %get-tuple-element.293, s32[512]{0:T(512)S(1)} %bitcast.128, s32[512]{0:T(512)S(1)} %bitcast.122, s32[512]{0:T(512)S(1)} %bitcast.123, s32[512]{0:T(512)S(1)} %bitcast.124, ...), kind=kOutput, calls=%fused_computation.53.clone.1 | convolution fusion | flops 692060160 | bytes 1860096 | tf_op jit(solution)/shard_map/while/body/eval_jaxpr/fc,tc->ft/dot_general | solution.py:84
  54.9 5.5 %fusion.72 = f32[8,256,512]{1,2,0:T(8,128)} fusion(f32[8,256,512]{1,2,0:T(8,128)} %get-tuple-element.276, s32[]{:T(128)} %get-tuple-element.275, bf16[256,2560]{1,0:T(8,128)(2,1)S(1)} %get-tuple-element.293, s32[512]{0:T(512)S(1)} %bitcast.128, s32[512]{0:T(512)S(1)} %bitcast.122, s32[512]{0:T(512)S(1)} %bitcast.123, s32[512]{0:T(512)S(1)} %bitcast.124, ...), kind=kOutput, calls=%fused_computation.53.clone.1 | convolution fusion | flops 692060160 | bytes 1860096 | tf_op jit(solution)/shard_map/while/body/eval_jaxpr/fc,tc->ft/dot_general | solution.py:84
  61.4 5.5 %fusion.72 = f32[8,256,512]{1,2,0:T(8,128)} fusion(f32[8,256,512]{1,2,0:T(8,128)} %get-tuple-element.276, s32[]{:T(128)} %get-tuple-element.275, bf16[256,2560]{1,0:T(8,128)(2,1)S(1)} %get-tuple-element.293, s32[512]{0:T(512)S(1)} %bitcast.128, s32[512]{0:T(512)S(1)} %bitcast.122, s32[512]{0:T(512)S(1)} %bitcast.123, s32[512]{0:T(512)S(1)} %bitcast.124, ...), kind=kOutput, calls=%fused_computation.53.clone.1 | convolution fusion | flops 692060160 | bytes 1860096 | tf_op jit(solution)/shard_map/while/body/eval_jaxpr/fc,tc->ft/dot_general | solution.py:84
  68.0 5.5 %fusion.72 = f32[8,256,512]{1,2,0:T(8,128)} fusion(f32[8,256,512]{1,2,0:T(8,128)} %get-tuple-element.276, s32[]{:T(128)} %get-tuple-element.275, bf16[256,2560]{1,0:T(8,128)(2,1)S(1)} %get-tuple-element.293, s32[512]{0:T(512)S(1)} %bitcast.128, s32[512]{0:T(512)S(1)} %bitcast.122, s32[512]{0:T(512)S(1)} %bitcast.123, s32[512]{0:T(512)S(1)} %bitcast.124, ...), kind=kOutput, calls=%fused_computation.53.clone.1 | convolution fusion | flops 692060160 | bytes 1860096 | tf_op jit(solution)/shard_map/while/body/eval_jaxpr/fc,tc->ft/dot_general | solution.py:84
  74.6 5.5 %fusion.72 = f32[8,256,512]{1,2,0:T(8,128)} fusion(f32[8,256,512]{1,2,0:T(8,128)} %get-tuple-element.276, s32[]{:T(128)} %get-tuple-element.275, bf16[256,2560]{1,0:T(8,128)(2,1)S(1)} %get-tuple-element.293, s32[512]{0:T(512)S(1)} %bitcast.128, s32[512]{0:T(512)S(1)} %bitcast.122, s32[512]{0:T(512)S(1)} %bitcast.123, s32[512]{0:T(512)S(1)} %bitcast.124, ...), kind=kOutput, calls=%fused_computation.53.clone.1 | convolution fusion | flops 692060160 | bytes 1860096 | tf_op jit(solution)/shard_map/while/body/eval_jaxpr/fc,tc->ft/dot_general | solution.py:84
  81.2 5.5 %fusion.72 = f32[8,256,512]{1,2,0:T(8,128)} fusion(f32[8,256,512]{1,2,0:T(8,128)} %get-tuple-element.276, s32[]{:T(128)} %get-tuple-element.275, bf16[256,2560]{1,0:T(8,128)(2,1)S(1)} %get-tuple-element.293, s32[512]{0:T(512)S(1)} %bitcast.128, s32[512]{0:T(512)S(1)} %bitcast.122, s32[512]{0:T(512)S(1)} %bitcast.123, s32[512]{0:T(512)S(1)} %bitcast.124, ...), kind=kOutput, calls=%fused_computation.53.clone.1 | convolution fusion | flops 692060160 | bytes 1860096 | tf_op jit(solution)/shard_map/while/body/eval_jaxpr/fc,tc->ft/dot_general | solution.py:84
  86.6 5.6 %copy.42 = f32[256,8,512]{2,1,0:T(8,128)} copy(f32[256,8,512]{0,2,1:T(8,128)} %bitcast.106) | data formatting | bytes 8388608 | tf_op jit(solution)/shard_map/transpose | solution.py:87
  92.2 5.1 %reshape.153 = f32[8,32,4096]{2,1,0:T(8,128)} reshape(f32[256,8,512]{2,1,0:T(8,128)} %copy.42) | data formatting | bytes 8388608 | tf_op jit(solution)/shard_map/reshape | solution.py:87
  97.3 2.5 %convert_element_type.23 = bf16[8,32,4096]{2,1,0:T(8,128)(2,1)S(1)} convert(f32[8,32,4096]{2,1,0:T(8,128)} %reshape.153) | non-fusion elementwise | flops 1048576 | bytes 6291456 | tf_op jit(solution)/shard_map/convert_element_type | solution.py:123
  100.0 4.8 %collective-permute-start.8 = (bf16[8,1,4096]{2,1,0:T(2,128)(2,1)S(1)}, bf16[8,1,4096]{2,1,0:T(2,128)(2,1)S(1)}, u32[]{:S(2)}, u32[]{:S(2)}) collective-permute-start(bf16[8,1,4096]{2,1,0:T(2,128)(2,1)S(1)} %get-tuple-element.134), channel_id=1, source_target_pairs={{0,1},{1,2},{2,3},{4,5},{5,6},{6,7},{8,9},{9,10},{10,11},{12,13},{... | collective-permute-start | bytes 196616 | tf_op jit(solution)/shard_map/ppermute | solution.py:30
  109.4 2.5 %collective-permute-start.5 = (f32[8,32,128]{2,1,0:T(8,128)S(1)}, f32[8,32,128]{2,1,0:T(8,128)S(1)}, u32[]{:S(2)}, u32[]{:S(2)}) collective-permute-start(f32[8,32,128]{2,1,0:T(8,128)S(1)} %get-tuple-element.133), channel_id=1, source_target_pairs={{4,0},{8,4},{12,8},{16,12},{20,16},{24,20},{28,24},{0,28},{5,1},{9... | collective-permute-start | bytes 393224 | tf_op jit(solution)/shard_map/ppermute | solution.py:33
  111.9 5.6 %copy.46 = f32[256,4096]{1,0:T(8,128)} copy(f32[256,4096]{0,1:T(8,128)} %bitcast.107) | data formatting | bytes 8388608 | tf_op jit(solution)/shard_map/concatenate | solution.py:34
  117.6 3.2 %maximum_convert_fusion = f32[8,34,4096]{2,1,0:T(8,128)} fusion(bf16[8,1,4096]{2,1,0:T(2,128)(2,1)S(1)} %collective-permute-done.9, bf16[8,32,4096]{2,1,0:T(8,128)(2,1)S(1)} %convert_element_type.23, bf16[8,1,4096]{2,1,0:T(2,128)(2,1)S(1)} %collective-permute-done.8), kind=kLoop, calls=%fused_computation.85 | loop fusion | flops 6684672 | bytes 6684672 | tf_op jit(solution)/shard_map/convert_element_type | solution.py:123
  120.8 2.4 %pad_maximum_fusion = f32[256,4352]{1,0:T(8,128)} fusion(f32[256,128]{1,0:T(8,128)S(1)} %bitcast.120, f32[256,4096]{1,0:T(8,128)S(1)} %copy-done, f32[256,128]{1,0:T(8,128)S(1)} %bitcast.119), kind=kLoop, calls=%fused_computation.79 | loop fusion | flops 2228224 | bytes 8912896 | tf_op jit(solution)/shard_map/concatenate | solution.py:34
  123.2 71.3 %while.21 = (s32[]{:T(128)}, f32[8,256,512]{2,1,0:T(8,128)}, s32[8]{0:T(128)S(1)}, f32[256,4352]{1,0:T(8,128)}, s32[8,6,512]{2,1,0:T(8,128)}, /*index=5*/f32[435...) while((s32[]{:T(128)}, f32[8,256,512]{2,1,0:T(8,128)}, ...), condition=%wide.region_5.6_spmd, body=%wide.region_3.5_spmd.sunk | while | flops 1221986816 | bytes 1901396 | solution.py:121
  127.2 4.9 %fusion.76 = f32[8,256,512]{2,1,0:T(8,128)} fusion(f32[8,256,512]{2,1,0:T(8,128)} %get-tuple-element.321, s32[]{:T(128)} %get-tuple-element.320, s32[512]{0:T(512)S(1)} %bitcast.140, s32[512]{0:T(512)S(1)} %bitcast.132, s32[512]{0:T(512)S(1)} %bitcast.134, s32[512]{0:T(512)S(1)} %bitcast.136, s32[512]{0:T(512)S(1)} %bitcast.138, ...), kind=kOutput, calls=%fused_computation.9.clone.1 | convolution fusion | flops 1214906368 | bytes 1852936 | tf_op jit(solution)/shard_map/while/body/eval_jaxpr/rc,tc->rt/dot_general | solution.py:112
  136.1 4.9 %fusion.76 = f32[8,256,512]{2,1,0:T(8,128)} fusion(f32[8,256,512]{2,1,0:T(8,128)} %get-tuple-element.321, s32[]{:T(128)} %get-tuple-element.320, s32[512]{0:T(512)S(1)} %bitcast.140, s32[512]{0:T(512)S(1)} %bitcast.132, s32[512]{0:T(512)S(1)} %bitcast.134, s32[512]{0:T(512)S(1)} %bitcast.136, s32[512]{0:T(512)S(1)} %bitcast.138, ...), kind=kOutput, calls=%fused_computation.9.clone.1 | convolution fusion | flops 1214906368 | bytes 1852936 | tf_op jit(solution)/shard_map/while/body/eval_jaxpr/rc,tc->rt/dot_general | solution.py:112
  145.0 4.9 %fusion.76 = f32[8,256,512]{2,1,0:T(8,128)} fusion(f32[8,256,512]{2,1,0:T(8,128)} %get-tuple-element.321, s32[]{:T(128)} %get-tuple-element.320, s32[512]{0:T(512)S(1)} %bitcast.140, s32[512]{0:T(512)S(1)} %bitcast.132, s32[512]{0:T(512)S(1)} %bitcast.134, s32[512]{0:T(512)S(1)} %bitcast.136, s32[512]{0:T(512)S(1)} %bitcast.138, ...), kind=kOutput, calls=%fused_computation.9.clone.1 | convolution fusion | flops 1214906368 | bytes 1852936 | tf_op jit(solution)/shard_map/while/body/eval_jaxpr/rc,tc->rt/dot_general | solution.py:112
  153.9 4.9 %fusion.76 = f32[8,256,512]{2,1,0:T(8,128)} fusion(f32[8,256,512]{2,1,0:T(8,128)} %get-tuple-element.321, s32[]{:T(128)} %get-tuple-element.320, s32[512]{0:T(512)S(1)} %bitcast.140, s32[512]{0:T(512)S(1)} %bitcast.132, s32[512]{0:T(512)S(1)} %bitcast.134, s32[512]{0:T(512)S(1)} %bitcast.136, s32[512]{0:T(512)S(1)} %bitcast.138, ...), kind=kOutput, calls=%fused_computation.9.clone.1 | convolution fusion | flops 1214906368 | bytes 1852936 | tf_op jit(solution)/shard_map/while/body/eval_jaxpr/rc,tc->rt/dot_general | solution.py:112
  162.8 4.9 %fusion.76 = f32[8,256,512]{2,1,0:T(8,128)} fusion(f32[8,256,512]{2,1,0:T(8,128)} %get-tuple-element.321, s32[]{:T(128)} %get-tuple-element.320, s32[512]{0:T(512)S(1)} %bitcast.140, s32[512]{0:T(512)S(1)} %bitcast.132, s32[512]{0:T(512)S(1)} %bitcast.134, s32[512]{0:T(512)S(1)} %bitcast.136, s32[512]{0:T(512)S(1)} %bitcast.138, ...), kind=kOutput, calls=%fused_computation.9.clone.1 | convolution fusion | flops 1214906368 | bytes 1852936 | tf_op jit(solution)/shard_map/while/body/eval_jaxpr/rc,tc->rt/dot_general | solution.py:112
  171.7 4.9 %fusion.76 = f32[8,256,512]{2,1,0:T(8,128)} fusion(f32[8,256,512]{2,1,0:T(8,128)} %get-tuple-element.321, s32[]{:T(128)} %get-tuple-element.320, s32[512]{0:T(512)S(1)} %bitcast.140, s32[512]{0:T(512)S(1)} %bitcast.132, s32[512]{0:T(512)S(1)} %bitcast.134, s32[512]{0:T(512)S(1)} %bitcast.136, s32[512]{0:T(512)S(1)} %bitcast.138, ...), kind=kOutput, calls=%fused_computation.9.clone.1 | convolution fusion | flops 1214906368 | bytes 1852936 | tf_op jit(solution)/shard_map/while/body/eval_jaxpr/rc,tc->rt/dot_general | solution.py:112
  180.6 4.9 %fusion.76 = f32[8,256,512]{2,1,0:T(8,128)} fusion(f32[8,256,512]{2,1,0:T(8,128)} %get-tuple-element.321, s32[]{:T(128)} %get-tuple-element.320, s32[512]{0:T(512)S(1)} %bitcast.140, s32[512]{0:T(512)S(1)} %bitcast.132, s32[512]{0:T(512)S(1)} %bitcast.134, s32[512]{0:T(512)S(1)} %bitcast.136, s32[512]{0:T(512)S(1)} %bitcast.138, ...), kind=kOutput, calls=%fused_computation.9.clone.1 | convolution fusion | flops 1214906368 | bytes 1852936 | tf_op jit(solution)/shard_map/while/body/eval_jaxpr/rc,tc->rt/dot_general | solution.py:112
  189.5 5.0 %fusion.76 = f32[8,256,512]{2,1,0:T(8,128)} fusion(f32[8,256,512]{2,1,0:T(8,128)} %get-tuple-element.321, s32[]{:T(128)} %get-tuple-element.320, s32[512]{0:T(512)S(1)} %bitcast.140, s32[512]{0:T(512)S(1)} %bitcast.132, s32[512]{0:T(512)S(1)} %bitcast.134, s32[512]{0:T(512)S(1)} %bitcast.136, s32[512]{0:T(512)S(1)} %bitcast.138, ...), kind=kOutput, calls=%fused_computation.9.clone.1 | convolution fusion | flops 1214906368 | bytes 1852936 | tf_op jit(solution)/shard_map/while/body/eval_jaxpr/rc,tc->rt/dot_general | solution.py:112
  194.5 6.6 %copy.44 = f32[256,8,512]{2,1,0:T(8,128)} copy(f32[256,8,512]{2,0,1:T(8,128)} %bitcast.109) | data formatting | bytes 8388608 | tf_op jit(solution)/shard_map/transpose | solution.py:122
  201.1 5.0 %reshape.155 = f32[8,32,4096]{2,1,0:T(8,128)} reshape(f32[256,8,512]{2,1,0:T(8,128)} %copy.44) | data formatting | bytes 8388608 | tf_op jit(solution)/shard_map/reshape | solution.py:122
  206.2 9.3 %fusion.49 = f32[8,32,4096]{2,1,0:T(8,128)} fusion(f32[8,34,4096]{2,1,0:T(8,128)} %maximum_convert_fusion, f32[8,32,4096]{2,1,0:T(8,128)} %reshape.153, f32[8,32,4096]{2,1,0:T(8,128)} %reshape.155, f32[8,32]{1,0:T(8,128)S(1)} %copy-done.4, f32[4096]{0:T(1024)S(1)} %convert_element_type.19), kind=kLoop, calls=%fused_computation.84 | loop fusion | flops 8388608 | bytes 20988928 | tf_op jit(solution)/shard_map/mul | solution.py:127
  (103 shorter events, 58.6 us)
Async XLA Ops:
  2.8 9.6 %copy-start.3 = (s32[4096]{0:T(1024)S(1)}, s32[4096]{0:T(1024)}, u32[]{:S(2)}) copy-start(s32[4096]{0:T(1024)} %param.18) | copy-start | bytes 49156
  2.8 13.8 %copy-start.1 = (f32[8,4096]{1,0:T(8,128)S(1)}, f32[8,4096]{1,0:T(8,128)}, u32[]{:S(2)}) copy-start(f32[8,4096]{1,0:T(8,128)} %param.15) | copy-start | bytes 393220
  2.8 13.8 %copy-start.2 = (s32[4096]{0:T(1024)S(1)}, s32[4096]{0:T(1024)}, u32[]{:S(2)}) copy-start(s32[4096]{0:T(1024)} %param.16) | copy-start | bytes 49156
  5.9 18.4 %collective-permute-start = (bf16[256,512]{0,1:T(8,128)(2,1)}, bf16[256,512]{0,1:T(8,128)(2,1)S(1)}, u32[]{:S(2)}, u32[]{:S(2)}) collective-permute-start(bf16[256,512]{0,1:T(8,128)(2,1)} %bitcast.26), channel_id=1, source_target_pairs={{0,24},{4,28},{8,0},{12,4},{16,8},{20,12},{24,16},{28,20},{1,25},{... | collective-permute-start | bytes 786440 | tf_op jit(solution)/shard_map/ppermute | solution.py:20
  10.4 14.1 %collective-permute-start.1 = (bf16[256,512]{0,1:T(8,128)(2,1)S(1)}, bf16[256,512]{0,1:T(8,128)(2,1)}, u32[]{:S(2)}, u32[]{:S(2)}) collective-permute-start(bf16[256,512]{0,1:T(8,128)(2,1)S(1)} %bitcast.115), channel_id=1, source_target_pairs={{0,28},{4,0},{8,4},{12,8},{16,12},{20,16},{24,20},{28,24},{1,29},{... | collective-permute-start | bytes 786440 | tf_op jit(solution)/shard_map/ppermute | solution.py:20
  12.0 13.7 %collective-permute-start.2 = (bf16[256,512]{0,1:T(8,128)(2,1)S(1)}, bf16[256,512]{0,1:T(8,128)(2,1)}, u32[]{:S(2)}, u32[]{:S(2)}) collective-permute-start(bf16[256,512]{0,1:T(8,128)(2,1)S(1)} %bitcast.114), channel_id=1, source_target_pairs={{0,4},{4,8},{8,12},{12,16},{16,20},{20,24},{24,28},{28,0},{1,5},{5... | collective-permute-start | bytes 786440 | tf_op jit(solution)/shard_map/ppermute | solution.py:20
  12.4 10.7 %collective-permute-start.6 = (f32[1,1,128]{2,1,0:T(1,128)S(1)}, f32[1,1,128]{2,1,0:T(1,128)S(1)}, u32[]{:S(2)}, u32[]{:S(2)}) collective-permute-start(f32[1,1,128]{2,1,0:T(1,128)S(1)} %get-tuple-element.141), channel_id=1, source_target_pairs={{0,4},{4,8},{8,12},{12,16},{16,20},{20,24},{24,28},{28,0},{1,5},{5... | collective-permute-start | bytes 1544 | tf_op jit(solution)/shard_map/ppermute | solution.py:30
  14.6 9.7 %collective-permute-start.7 = (f32[1,1,128]{2,1,0:T(1,128)S(1)}, f32[1,1,128]{2,1,0:T(1,128)S(1)}, u32[]{:S(2)}, u32[]{:S(2)}) collective-permute-start(f32[1,1,128]{2,1,0:T(1,128)S(1)} %get-tuple-element.142), channel_id=1, source_target_pairs={{4,0},{8,4},{12,8},{16,12},{20,16},{24,20},{28,24},{0,28},{5,1},{9... | collective-permute-start | bytes 1544 | tf_op jit(solution)/shard_map/ppermute | solution.py:33
  23.1 9.3 %collective-permute-start.3 = (bf16[256,512]{0,1:T(8,128)(2,1)S(1)}, bf16[256,512]{0,1:T(8,128)(2,1)S(1)}, u32[]{:S(2)}, u32[]{:S(2)}) collective-permute-start(bf16[256,512]{0,1:T(8,128)(2,1)S(1)} %bitcast.116), channel_id=1, source_target_pairs={{0,8},{4,12},{8,16},{12,20},{16,24},{20,28},{24,0},{28,4},{1,9},{5... | collective-permute-start | bytes 786440 | tf_op jit(solution)/shard_map/ppermute | solution.py:20
  100.0 17.5 %collective-permute-start.8 = (bf16[8,1,4096]{2,1,0:T(2,128)(2,1)S(1)}, bf16[8,1,4096]{2,1,0:T(2,128)(2,1)S(1)}, u32[]{:S(2)}, u32[]{:S(2)}) collective-permute-start(bf16[8,1,4096]{2,1,0:T(2,128)(2,1)S(1)} %get-tuple-element.134), channel_id=1, source_target_pairs={{0,1},{1,2},{2,3},{4,5},{5,6},{6,7},{8,9},{9,10},{10,11},{12,13},{... | collective-permute-start | bytes 196616 | tf_op jit(solution)/shard_map/ppermute | solution.py:30
  104.8 12.8 %collective-permute-start.9 = (bf16[8,1,4096]{2,1,0:T(2,128)(2,1)S(1)}, bf16[8,1,4096]{2,1,0:T(2,128)(2,1)S(1)}, u32[]{:S(2)}, u32[]{:S(2)}) collective-permute-start(bf16[8,1,4096]{2,1,0:T(2,128)(2,1)S(1)} %get-tuple-element.135), channel_id=1, source_target_pairs={{1,0},{2,1},{3,2},{5,4},{6,5},{7,6},{9,8},{10,9},{11,10},{13,12},{... | collective-permute-start | bytes 196616 | tf_op jit(solution)/shard_map/ppermute | solution.py:33
  107.7 13.1 %collective-permute-start.4 = (f32[8,32,128]{2,1,0:T(8,128)S(1)}, f32[8,32,128]{2,1,0:T(8,128)S(1)}, u32[]{:S(2)}, u32[]{:S(2)}) collective-permute-start(f32[8,32,128]{2,1,0:T(8,128)S(1)} %get-tuple-element.132), channel_id=1, source_target_pairs={{0,4},{4,8},{8,12},{12,16},{16,20},{20,24},{24,28},{28,0},{1,5},{5... | collective-permute-start | bytes 393224 | tf_op jit(solution)/shard_map/ppermute | solution.py:30
  109.4 11.4 %collective-permute-start.5 = (f32[8,32,128]{2,1,0:T(8,128)S(1)}, f32[8,32,128]{2,1,0:T(8,128)S(1)}, u32[]{:S(2)}, u32[]{:S(2)}) collective-permute-start(f32[8,32,128]{2,1,0:T(8,128)S(1)} %get-tuple-element.133), channel_id=1, source_target_pairs={{4,0},{8,4},{12,8},{16,12},{20,16},{24,20},{28,24},{0,28},{5,1},{9... | collective-permute-start | bytes 393224 | tf_op jit(solution)/shard_map/ppermute | solution.py:33
  117.5 3.2 %copy-start = (f32[256,4096]{1,0:T(8,128)S(1)}, f32[256,4096]{1,0:T(8,128)}, u32[]{:S(2)}) copy-start(f32[256,4096]{1,0:T(8,128)} %copy.46) | copy-start | bytes 12582916
  201.1 5.0 %copy-start.4 = (f32[8,32]{1,0:T(8,128)S(1)}, f32[8,32]{1,0:T(8,128)}, u32[]{:S(2)}) copy-start(f32[8,32]{1,0:T(8,128)} %param.19) | copy-start | bytes 3076
where the time goes:
time: 218 us; the launch traced here: 215 us
  matrix products  84.6 us (39%)
  local copies, waits for them, and re-layouts  53.4 us (24%)
  other arithmetic  38.6 us (18%)
  starting transfers between devices  22 us (10%)
  waiting for transfers between devices  11.2 us (5%)
  loops' own time  5.42 us (2%)
    dot_general x8, matrix products, remap_block(): jnp.einsum('fc,tc->ft', received, dense, preferred_element_type=jnp.float32)  43.7 us
    dot_general x8, matrix products, stencil_block(): jnp.einsum('rc,tc->rt', field_window, weights, precision=lax.Precision.HI...  39.5 us
    reduce_sum x8, other arithmetic, stencil_block(): return gathered - jnp.sum(weights, axis=1)[None, :] * own  13.4 us
    mul x1, other arithmetic, on_device(): ocean[None, None, :]  9.26 us
    ppermute x3, starting transfers between devices, extended(): lax.ppermute(lax.slice_in_dim(block, block.shape[dim] - width, None, axis...  8.66 us
    slice x8, local copies, waits for them, and re-layouts, remap_block(): block_cols[slot][:, None] == column_ids  8.19 us
    sub x8, other arithmetic, stencil_block(): local_pos = near[neighbour] - start  7.65 us
    ppermute x4, starting transfers between devices, passed_along(): return lax.ppermute(value, axis, pairs)  6.91 us
  transfers between devices with their start and end apart: 10, of which 2 were waited for; matrix products, arithmetic and copies ran while one was open for 6% of the time, Pallas kernels for 0%

commit v1 on v0

v1 whole, which is shorter than its diff:
```python
import functools

import jax
import jax.numpy as jnp
from jax import lax
from jax.experimental import pallas as pl
from jax.experimental.pallas import tpu as pltpu
from jax.sharding import PartitionSpec as P

B = 128
CAP = 4
R = 2
K = 8
NN = 6
H = 128
OFFS = 2 * R + 1
SET = CAP * B
HALF = 256
TILE = 256
MESH = pl.DeviceIdType.MESH
vertical_rate = 0.1
ORDER = (R + 1, R - 1, R + 2, R - 2)


def kernel(
    fields,
    levels,
    slots_ref,
    src_ref,
    col_ref,
    wt_ref,
    cnt_ref,
    near_ref,
    land_ref,
    diff_ref,
    out_ref,
    blocks,
    outbox,
    inbox,
    d0,
    d1,
    d2,
    d3,
    d4,
    wref,
    share_ref,
    rref,
    xm,
    tri_ref,
    dref,
    lev_out,
    lev_in,
    send_sem,
    recv_sem,
    halo_send,
    halo_recv,
    lev_send,
    lev_recv,
    out_sem,
):
    dense = (d0, d1, d2, d3, d4)
    rows = fields * levels
    targets = land_ref.shape[1]
    tiles = targets // TILE
    f32, bf16 = jnp.float32, jnp.bfloat16
    nd = lax.axis_size("dom")
    nl = lax.axis_size("lev")
    me = lax.axis_index("dom")
    lev = lax.axis_index("lev")

    def at(step):
        return lax.rem(me + step + nd, nd)

    barrier = pltpu.get_barrier_semaphore()
    for step in (-2, -1, 1, 2):
        pl.semaphore_signal(barrier, inc=1, device_id=(at(step), lev), device_id_type=MESH)

    @pl.when(lev > 0)
    def _():
        pl.semaphore_signal(barrier, inc=1, device_id=(me, lev - 1), device_id_type=MESH)

    @pl.when(lev < nl - 1)
    def _():
        pl.semaphore_signal(barrier, inc=1, device_id=(me, lev + 1), device_id_type=MESH)

    def pick(offset):
        for c in range(CAP):
            slot = slots_ref[0, offset, c]
            outbox[offset, :, c * B : (c + 1) * B] = blocks[slot]

    for block in range(src_ref.shape[1] // B):
        blocks[block] = src_ref[:, block * B : (block + 1) * B]
    for offset in ORDER:
        pick(offset)
    beside_count = jnp.where(lev > 0, 1, 0) + jnp.where(lev < nl - 1, 1, 0)
    pl.semaphore_wait(barrier, 4 + beside_count)

    copies = []
    for i, offset in enumerate(ORDER):
        copy = pltpu.make_async_remote_copy(
            src_ref=outbox.at[offset],
            dst_ref=inbox.at[i],
            send_sem=send_sem.at[i],
            recv_sem=recv_sem.at[i],
            device_id=(at(offset - R), lev),
            device_id_type=MESH,
        )
        copy.start()
        copies.append(copy)
    pick(R)

    slot_ids = lax.broadcasted_iota(jnp.int32, (K, targets), 0)
    live = jnp.where(slot_ids < cnt_ref[...], wt_ref[...], 0.0)
    share_ref[...] = (live / jnp.sum(live, axis=0, keepdims=True)).astype(bf16).astype(f32)

    row16 = lax.broadcasted_iota(jnp.int32, (16, B), 0).astype(f32)

    def strip_of(s):
        return pl.ds(pl.multiple_of(s * B, B), B)

    def build(offset, s):
        target = dense[offset]
        lanes = strip_of(s)
        col = col_ref[:, lanes].astype(f32)
        share = share_ref[:, lanes]
        shares = [jnp.broadcast_to(share[k : k + 1], (16, B)).astype(bf16) for k in range(K)]
        for h in range(SET // HALF):
            base = float(offset * SET + h * HALF)
            places = [
                jnp.broadcast_to(col[k : k + 1] - base, (16, B)).astype(bf16) for k in range(K)
            ]
            for i in range(HALF // 16):
                ids = (row16 + float(16 * i)).astype(bf16)
                acc = jnp.zeros((16, B), bf16)
                for k in range(K):
                    acc = jnp.where(places[k] == ids, shares[k], acc)
                start = h * HALF + 16 * i
                target[start : start + 16, lanes] = acc

    def build_near(s):
        lanes = strip_of(s)
        start = (s // (TILE // B)) * TILE
        near = (near_ref[:, lanes] - start).astype(f32)
        one = jnp.ones((16, B), bf16)
        for h in range(2):
            places = [
                jnp.broadcast_to(near[n : n + 1] - float(h * HALF), (16, B)).astype(bf16)
                for n in range(NN)
            ]
            for i in range(HALF // 16):
                ids = (row16 + float(16 * i)).astype(bf16)
                acc = jnp.zeros((16, B), bf16)
                for n in range(NN):
                    acc = jnp.where(places[n] == ids, acc + one, acc)
                at_row = h * HALF + 16 * i
                wref[at_row : at_row + 16, lanes] = acc

    def tile_of(j, shift=0, width=TILE):
        return pl.ds(pl.multiple_of(j * TILE + shift, B), width)

    def product(offset, j):
        left = outbox[R] if offset == R else inbox[ORDER.index(offset)]
        return jnp.dot(left, dense[offset][:, tile_of(j)], preferred_element_type=f32)

    def loop(body, low, high):
        lax.fori_loop(low, high, lambda j, c: (body(j), c)[1], 0)

    both = TILE // B

    def build_tile(offset, j):
        for p in range(both):
            build(offset, j * both + p)

    def near_tile(j):
        for p in range(both):
            build_near(j * both + p)

    for part in range(rows // TILE):
        row_id = lax.broadcasted_iota(jnp.int32, (TILE, rows), 0) + part * TILE
        col_id = lax.broadcasted_iota(jnp.int32, (TILE, rows), 1)
        beside = (jnp.abs(row_id - col_id) == 1) & (row_id // levels == col_id // levels)
        tri_ref[part * TILE : (part + 1) * TILE, :] = jnp.where(beside, 1.0, 0.0).astype(bf16)
    lane_id = lax.broadcasted_iota(jnp.int32, (levels, levels), 1)
    level_id = lax.broadcasted_iota(jnp.int32, (levels, levels), 0)
    for f in range(fields):
        spread = jnp.broadcast_to(diff_ref[f : f + 1, :], (levels, levels))
        column = jnp.sum(jnp.where(lane_id == level_id, spread, 0.0), axis=1, keepdims=True)
        dref[f * levels : (f + 1) * levels, :] = jnp.broadcast_to(column, (levels, TILE))
    first_row = lax.broadcasted_iota(jnp.int32, (16, targets), 0) == 0
    ocean_row = jnp.broadcast_to(land_ref[...].astype(f32), (16, targets))
    xm[rows:, H : H + targets] = jnp.where(first_row, ocean_row, 0.0).astype(bf16)

    def own_first(j):
        rref[:, tile_of(j)] = product(R, j)
        build_tile(ORDER[0], j)

    def add_and_build(offset, following):
        def body(j):
            rref[:, tile_of(j)] += product(offset, j)
            build_tile(following, j)

        return body

    def add(offset):
        def body(j):
            rref[:, tile_of(j)] += product(offset, j)

        return body

    loop(lambda j: build_tile(R, j), 0, tiles)
    loop(own_first, 0, tiles)
    loop(near_tile, 0, tiles)
    loop(lambda j: build_tile(ORDER[1], j), 0, tiles)
    copies[0].wait_recv()
    loop(add_and_build(ORDER[0], ORDER[2]), 0, tiles)
    copies[1].wait_recv()
    loop(add_and_build(ORDER[1], ORDER[3]), 0, tiles)
    copies[2].wait_recv()
    loop(add(ORDER[2]), 0, tiles)
    copies[3].wait_recv()

    def last(j):
        value = rref[:, tile_of(j)] + product(ORDER[3], j)
        rref[:, tile_of(j)] = value
        ocean = land_ref[:, tile_of(j)].astype(f32)
        xm[:rows, tile_of(j, H)] = (value * ocean).astype(bf16)
        for side, level in ((0, levels - 1), (1, 0)):
            picked = [
                rref[f * levels + level : f * levels + level + 1, tile_of(j, p * B, B)]
                for p in range(both)
                for f in range(fields)
            ]
            lev_out[side, :, strip_of(j)] = jnp.concatenate(picked, axis=0).astype(bf16)

    last(0)
    last(tiles - 1)
    halos = []
    for i, (start, landing, step) in enumerate(
        ((targets, 0, 1), (H, H + targets, -1))
    ):
        copy = pltpu.make_async_remote_copy(
            src_ref=xm.at[:, pl.ds(start, H)],
            dst_ref=xm.at[:, pl.ds(landing, H)],
            send_sem=halo_send.at[i],
            recv_sem=halo_recv.at[i],
            device_id=(at(step), lev),
            device_id_type=MESH,
        )
        copy.start()
        halos.append(copy)
    loop(last, 1, tiles - 1)

    def level_copy(side):
        return pltpu.make_async_remote_copy(
            src_ref=lev_out.at[side],
            dst_ref=lev_in.at[side],
            send_sem=lev_send.at[side],
            recv_sem=lev_recv.at[side],
            device_id=(me, lev + 1 if side == 0 else lev - 1),
            device_id_type=MESH,
        )

    @pl.when(lev < nl - 1)
    def _():
        level_copy(0).start()

    @pl.when(lev > 0)
    def _():
        level_copy(1).start()

    @pl.when(lev == 0)
    def _():
        lev_in[0] = jnp.zeros(lev_in.shape[1:], bf16)

    @pl.when(lev == nl - 1)
    def _():
        lev_in[1] = jnp.zeros(lev_in.shape[1:], bf16)

    def final(j):
        gathered = jnp.dot(
            xm[:, tile_of(j, 0, 2 * TILE)], wref[:, tile_of(j)], preferred_element_type=f32
        )
        value = rref[:, tile_of(j)]
        beside = jnp.dot(tri_ref[...], value.astype(bf16), preferred_element_type=f32)
        d = dref[...]
        total = gathered[rows : rows + 1]
        rref[:, tile_of(j)] = (
            value * ((1.0 - 2.0 * vertical_rate) - d * total)
            + d * gathered[:rows]
            + vertical_rate * beside
        )

    def out_copy(j):
        return pltpu.make_async_copy(
            rref.at[:, tile_of(j)], out_ref.at[:, tile_of(j)], out_sem.at[j]
        )

    def edges(j):
        for side, level in ((0, 0), (1, levels - 1)):
            part = lev_in[side, :, strip_of(j)].astype(f32)
            for p in range(both):
                for f in range(fields):
                    row = f * levels + level
                    at_part = p * fields + f
                    edge = part[at_part : at_part + 1]
                    rref[row : row + 1, tile_of(j, p * B, B)] += vertical_rate * edge
        out_copy(j).start()

    loop(final, 1, tiles - 1)
    for copy in halos:
        copy.wait_recv()
    for copy in halos:
        copy.wait_send()
    final(0)
    final(tiles - 1)

    @pl.when(lev > 0)
    def _():
        level_copy(0).wait_recv()
        level_copy(1).wait_send()

    @pl.when(lev < nl - 1)
    def _():
        level_copy(1).wait_recv()
        level_copy(0).wait_send()

    loop(edges, 0, tiles)
    for copy in copies:
        copy.wait_send()
    loop(lambda j: out_copy(j).wait(), 0, tiles)


def on_device(
    source,
    send_slots,
    intersection_col,
    intersection_wt,
    intersection_count,
    neighbours,
    land_mask,
    diffusivity,
):
    fields, levels, columns = source.shape
    rows = fields * levels
    targets = land_mask.shape[0]
    f32, bf16 = jnp.float32, jnp.bfloat16
    vmem = pl.BlockSpec(memory_space=pltpu.VMEM)
    land = land_mask.reshape(1, targets)
    result = pl.pallas_call(
        functools.partial(kernel, fields, levels),
        out_shape=jax.ShapeDtypeStruct((rows, targets), f32),
        in_specs=[pl.BlockSpec(memory_space=pltpu.SMEM)] + [vmem] * 7,
        out_specs=pl.BlockSpec(memory_space=pl.ANY),
        scratch_shapes=[
            pltpu.VMEM((columns // B, rows, B), bf16),
            pltpu.VMEM((OFFS, rows, SET), bf16),
            pltpu.VMEM((OFFS - 1, rows, SET), bf16),
        ]
        + [pltpu.VMEM((SET, targets), bf16) for _ in range(OFFS)]
        + [
            pltpu.VMEM((2 * TILE, targets), bf16),
            pltpu.VMEM((K, targets), f32),
            pltpu.VMEM((rows, targets), f32),
            pltpu.VMEM((rows + 16, targets + 2 * H), bf16),
            pltpu.VMEM((rows, rows), bf16),
            pltpu.VMEM((rows, TILE), f32),
            pltpu.VMEM((2, 2 * fields, targets // 2), bf16),
            pltpu.VMEM((2, 2 * fields, targets // 2), bf16),
            pltpu.SemaphoreType.DMA((OFFS - 1,)),
            pltpu.SemaphoreType.DMA((OFFS - 1,)),
            pltpu.SemaphoreType.DMA((2,)),
            pltpu.SemaphoreType.DMA((2,)),
            pltpu.SemaphoreType.DMA((2,)),
            pltpu.SemaphoreType.DMA((2,)),
            pltpu.SemaphoreType.DMA((targets // TILE,)),
        ],
        compiler_params=pltpu.CompilerParams(
            collective_id=0, has_side_effects=True, vmem_limit_bytes=48 * 1024 * 1024
        ),
    )(
        send_slots,
        source.reshape(rows, columns),
        intersection_col,
        intersection_wt,
        intersection_count.reshape(1, targets),
        neighbours,
        land,
        diffusivity,
    )
    updated = land.astype(f32) * result
    return updated.reshape(fields, levels, targets)


def solution(mesh):
    return jax.shard_map(
        on_device,
        mesh=mesh,
        in_specs=(
            P(None, "lev", "dom"),
            P("dom", None, None),
            P(None, "dom"),
            P(None, "dom"),
            P("dom"),
            P(None, "dom"),
            P("dom"),
            P(None, "lev"),
        ),
        out_specs=P(None, "lev", "dom"),
        check_vma=False,
    )
```

time: 218 us -> 60.4 us (0.28)
  the two profiles are of different devices: /device:TPU:1 before, /device:TPU:0 now
where the time goes in v1:
time: 60.4 us; the launch traced here: 60 us
  Pallas kernels  50.6 us (84%)
  local copies, waits for them, and re-layouts  6.82 us (11%)
  other arithmetic  2.49 us (4%)
    pallas_call x1, Pallas kernels, on_device(): pl.pallas_call(functools.partial(kernel, fields, levels), out_shape=jax.S...  50.6 us
    unnamed x15, local copies, waits for them, and re-layouts  6.82 us
    mul x1, other arithmetic, on_device(): updated = land.astype(f32) * result  2.49 us

profile of v1, /device:TPU:0, one launch (start us, length us, event | category | flops | bytes accessed | tf_op | source)
XLA Modules:
  0.0 60.0 jit_solution(17190940300103203514)
XLA Ops:
  0.0 0.8 %copy.9.slots_ref = s32[1,5,4]{2,1,0:T(8,128)S(1)} copy(s32[1,5,4]{1,2,0:T(4,128)} %param.9) | data formatting | bytes 160 | tf_op args[1]
  0.8 0.0 copy-start
  0.8 1.2 %copy-done = bf16[8,32,2048]{2,1,0:T(8,128)(2,1)S(1)} copy-done((bf16[8,32,2048]{2,1,0:T(8,128)(2,1)S(1)}, bf16[8,32,2048]{2,1,0:T(8,128)(2,1)}, u32[]{:S(2)}) %copy-start) | copy-done | bytes 1048600
  2.0 0.0 copy-start.1
  2.0 0.9 %copy-done.1 = s32[8,4096]{1,0:T(8,128)S(1)} copy-done((s32[8,4096]{1,0:T(8,128)S(1)}, s32[8,4096]{1,0:T(8,128)}, u32[]{:S(2)}) %copy-start.1) | copy-done | bytes 131096
  2.9 0.0 copy-start.2
  2.9 0.9 %copy-done.2 = f32[8,4096]{1,0:T(8,128)S(1)} copy-done((f32[8,4096]{1,0:T(8,128)S(1)}, f32[8,4096]{1,0:T(8,128)}, u32[]{:S(2)}) %copy-start.2) | copy-done | bytes 131096
  3.8 0.0 copy-start.3
  3.8 0.9 %copy-done.3 = s32[6,4096]{1,0:T(8,128)S(1)} copy-done((s32[6,4096]{1,0:T(8,128)S(1)}, s32[6,4096]{1,0:T(8,128)}, u32[]{:S(2)}) %copy-start.3) | copy-done | bytes 98328
  4.7 0.0 copy-start.4
  4.7 0.7 %copy-done.4 = s32[4096]{0:T(1024)S(1)} copy-done((s32[4096]{0:T(1024)S(1)}, s32[4096]{0:T(1024)}, u32[]{:S(2)}) %copy-start.4) | copy-done | bytes 16408
  5.4 0.0 copy-start.5
  5.4 0.7 %copy-done.5 = s32[4096]{0:T(1024)S(1)} copy-done((s32[4096]{0:T(1024)S(1)}, s32[4096]{0:T(1024)}, u32[]{:S(2)}) %copy-start.5) | copy-done | bytes 16408
  6.1 0.0 copy-start.6
  6.1 0.7 %copy-done.6 = f32[8,32]{1,0:T(8,128)S(1)} copy-done((f32[8,32]{1,0:T(8,128)S(1)}, f32[8,32]{1,0:T(8,128)}, u32[]{:S(2)}) %copy-start.6) | copy-done | bytes 1048
  6.8 50.6 %shard_map.82 = f32[256,4096]{1,0:T(8,128)S(1)} custom-call(s32[1,5,4]{2,1,0:T(8,128)S(1)} %copy.9.slots_ref, bf16[256,2048]{1,0:T(8,128)(2,1)S(1)} %bitcast.4, s32[8,4096]{1,0:T(8,128)S(1)} %copy-done.1, f32[8,4096]{1,0:T(8,128)S(1)} %copy-done.2, s32[1,4096]{1,0:T(1,128)S(1)} %bitcast.6, s32[6,4096]{1,0:T(8,128)S(1)} %copy-done.3, s32[1,4096]{1,0:T(1,128)S(1)} %bitcast.5, ...), custom_call_target="tpu_custom_call" | custom-call | tf_op jit(solution)/shard_map/pallas_call | solution.py:349
  57.5 2.5 %broadcast_multiply_fusion = f32[256,4096]{1,0:T(8,128)} fusion(f32[256,4096]{1,0:T(8,128)S(1)} %shard_map.82, f32[4096]{0:T(1024)S(1)} %convert_element_type.4), kind=kLoop, calls=%fused_computation | loop fusion | flops 1048576 | bytes 8404992 | tf_op jit(solution)/shard_map/mul | solution.py:390
  (1 shorter events, 0.0 us)
Async XLA Ops:
  0.8 1.2 %copy-start = (bf16[8,32,2048]{2,1,0:T(8,128)(2,1)S(1)}, bf16[8,32,2048]{2,1,0:T(8,128)(2,1)}, u32[]{:S(2)}) copy-start(bf16[8,32,2048]{2,1,0:T(8,128)(2,1)} %param.8) | copy-start | bytes 3145732
  2.0 0.9 %copy-start.1 = (s32[8,4096]{1,0:T(8,128)S(1)}, s32[8,4096]{1,0:T(8,128)}, u32[]{:S(2)}) copy-start(s32[8,4096]{1,0:T(8,128)} %col_ref.1) | copy-start | bytes 393220
  2.9 0.9 %copy-start.2 = (f32[8,4096]{1,0:T(8,128)S(1)}, f32[8,4096]{1,0:T(8,128)}, u32[]{:S(2)}) copy-start(f32[8,4096]{1,0:T(8,128)} %wt_ref.1) | copy-start | bytes 393220
  3.8 0.9 %copy-start.3 = (s32[6,4096]{1,0:T(8,128)S(1)}, s32[6,4096]{1,0:T(8,128)}, u32[]{:S(2)}) copy-start(s32[6,4096]{1,0:T(8,128)} %near_ref.1) | copy-start | bytes 294916
  4.7 0.7 %copy-start.4 = (s32[4096]{0:T(1024)S(1)}, s32[4096]{0:T(1024)}, u32[]{:S(2)}) copy-start(s32[4096]{0:T(1024)} %param.14) | copy-start | bytes 49156
  5.4 0.7 %copy-start.5 = (s32[4096]{0:T(1024)S(1)}, s32[4096]{0:T(1024)}, u32[]{:S(2)}) copy-start(s32[4096]{0:T(1024)} %param.12) | copy-start | bytes 49156
  6.1 0.7 %copy-start.6 = (f32[8,32]{1,0:T(8,128)S(1)}, f32[8,32]{1,0:T(8,128)}, u32[]{:S(2)}) copy-start(f32[8,32]{1,0:T(8,128)} %diff_ref.1) | copy-start | bytes 3076

commit v2 on v1

--- a/solution.py
+++ b/solution.py
@@ -25,6 +25,15 @@
 def kernel(
     fields,
     levels,
+    slots_hbm,
+    src_hbm,
+    col_hbm,
+    wt_hbm,
+    cnt_hbm,
+    near_hbm,
+    land_hbm,
+    diff_hbm,
+    out_ref,
     slots_ref,
     src_ref,
     col_ref,
@@ -33,15 +42,13 @@
     near_ref,
     land_ref,
     diff_ref,
-    out_ref,
+    in_sem,
     blocks,
     outbox,
     inbox,
-    d0,
-    d1,
-    d2,
-    d3,
-    d4,
+    own_dense,
+    near_dense,
+    far_dense,
     wref,
     share_ref,
     rref,
@@ -58,7 +65,25 @@
     lev_recv,
     out_sem,
 ):
-    dense = (d0, d1, d2, d3, d4)
+    loads = []
+    for i, (hbm, ref) in enumerate(
+        (
+            (src_hbm, src_ref),
+            (slots_hbm, slots_ref),
+            (col_hbm, col_ref),
+            (wt_hbm, wt_ref),
+            (cnt_hbm, cnt_ref),
+            (near_hbm, near_ref),
+            (land_hbm, land_ref),
+            (diff_hbm, diff_ref),
+        )
+    ):
+        load = pltpu.make_async_copy(hbm, ref, in_sem.at[i])
+        load.start()
+        loads.append(load)
+    dense = {R: (own_dense, 0)}
+    for i, offset in enumerate(ORDER):
+        dense[offset] = ((near_dense, far_dense)[i // 2], (i % 2) * SET)
     rows = fields * levels
     targets = land_ref.shape[1]
     tiles = targets // TILE
@@ -88,6 +113,8 @@
             slot = slots_ref[0, offset, c]
             outbox[offset, :, c * B : (c + 1) * B] = blocks[slot]
 
+    loads[0].wait()
+    loads[1].wait()
     for block in range(src_ref.shape[1] // B):
         blocks[block] = src_ref[:, block * B : (block + 1) * B]
     for offset in ORDER:
@@ -99,7 +126,7 @@
     for i, offset in enumerate(ORDER):
         copy = pltpu.make_async_remote_copy(
             src_ref=outbox.at[offset],
-            dst_ref=inbox.at[i],
+            dst_ref=inbox.at[i // 2, :, pl.ds((i % 2) * SET, SET)],
             send_sem=send_sem.at[i],
             recv_sem=recv_sem.at[i],
             device_id=(at(offset - R), lev),
@@ -109,6 +136,8 @@
         copies.append(copy)
     pick(R)
 
+    for load in loads[2:]:
+        load.wait()
     slot_ids = lax.broadcasted_iota(jnp.int32, (K, targets), 0)
     live = jnp.where(slot_ids < cnt_ref[...], wt_ref[...], 0.0)
     share_ref[...] = (live / jnp.sum(live, axis=0, keepdims=True)).astype(bf16).astype(f32)
@@ -119,7 +148,7 @@
         return pl.ds(pl.multiple_of(s * B, B), B)
 
     def build(offset, s):
-        target = dense[offset]
+        target, low_row = dense[offset]
         lanes = strip_of(s)
         col = col_ref[:, lanes].astype(f32)
         share = share_ref[:, lanes]
@@ -134,7 +163,7 @@
                 acc = jnp.zeros((16, B), bf16)
                 for k in range(K):
                     acc = jnp.where(places[k] == ids, shares[k], acc)
-                start = h * HALF + 16 * i
+                start = low_row + h * HALF + 16 * i
                 target[start : start + 16, lanes] = acc
 
     def build_near(s):
@@ -158,12 +187,20 @@
     def tile_of(j, shift=0, width=TILE):
         return pl.ds(pl.multiple_of(j * TILE + shift, B), width)
 
-    def product(offset, j):
-        left = outbox[R] if offset == R else inbox[ORDER.index(offset)]
-        return jnp.dot(left, dense[offset][:, tile_of(j)], preferred_element_type=f32)
-
-    def loop(body, low, high):
-        lax.fori_loop(low, high, lambda j, c: (body(j), c)[1], 0)
+    def product(part, j):
+        if part == 0:
+            left, right = outbox[R], own_dense
+        else:
+            left, right = inbox[part - 1], (near_dense, far_dense)[part - 1]
+        return jnp.dot(left, right[:, tile_of(j)], preferred_element_type=f32)
+
+    def loop(body, low, high, group=1):
+        def step(i, carry):
+            for p in range(group):
+                body(low + i * group + p)
+            return carry
+
+        lax.fori_loop(0, (high - low) // group, step, 0)
 
     both = TILE // B
 
@@ -191,36 +228,26 @@
     xm[rows:, H : H + targets] = jnp.where(first_row, ocean_row, 0.0).astype(bf16)
 
     def own_first(j):
-        rref[:, tile_of(j)] = product(R, j)
+        rref[:, tile_of(j)] = product(0, j)
         build_tile(ORDER[0], j)
 
-    def add_and_build(offset, following):
-        def body(j):
-            rref[:, tile_of(j)] += product(offset, j)
-            build_tile(following, j)
-
-        return body
-
-    def add(offset):
-        def body(j):
-            rref[:, tile_of(j)] += product(offset, j)
-
-        return body
+    def second(j):
+        rref[:, tile_of(j)] += product(1, j)
+        build_tile(ORDER[3], j)
 
     loop(lambda j: build_tile(R, j), 0, tiles)
-    loop(own_first, 0, tiles)
+    loop(own_first, 0, tiles, 2)
     loop(near_tile, 0, tiles)
     loop(lambda j: build_tile(ORDER[1], j), 0, tiles)
+    loop(lambda j: build_tile(ORDER[2], j), 0, tiles)
     copies[0].wait_recv()
-    loop(add_and_build(ORDER[0], ORDER[2]), 0, tiles)
     copies[1].wait_recv()
-    loop(add_and_build(ORDER[1], ORDER[3]), 0, tiles)
+    loop(second, 0, tiles, 2)
     copies[2].wait_recv()
-    loop(add(ORDER[2]), 0, tiles)
     copies[3].wait_recv()
 
     def last(j):
-        value = rref[:, tile_of(j)] + product(ORDER[3], j)
+        value = rref[:, tile_of(j)] + product(2, j)
         rref[:, tile_of(j)] = value
         ocean = land_ref[:, tile_of(j)].astype(f32)
         xm[:rows, tile_of(j, H)] = (value * ocean).astype(bf16)
@@ -248,7 +275,7 @@
         )
         copy.start()
         halos.append(copy)
-    loop(last, 1, tiles - 1)
+    loop(last, 1, tiles - 1, 2)
 
     def level_copy(side):
         return pltpu.make_async_remote_copy(
@@ -306,25 +333,31 @@
                     rref[row : row + 1, tile_of(j, p * B, B)] += vertical_rate * edge
         out_copy(j).start()
 
-    loop(final, 1, tiles - 1)
+    middle = tiles // 2 - 1
+    loop(final, 1, middle, 2)
+
+    @pl.when(lev > 0)
+    def _():
+        level_copy(0).wait_recv()
+        level_copy(1).wait_send()
+
+    @pl.when(lev < nl - 1)
+    def _():
+        level_copy(1).wait_recv()
+        level_copy(0).wait_send()
+
+    def finish(j):
+        final(j)
+        edges(j)
+
+    loop(edges, 1, middle)
+    loop(finish, middle, tiles - 1, 2)
     for copy in halos:
         copy.wait_recv()
     for copy in halos:
         copy.wait_send()
-    final(0)
-    final(tiles - 1)
-
-    @pl.when(lev > 0)
-    def _():
-        level_copy(0).wait_recv()
-        level_copy(1).wait_send()
-
-    @pl.when(lev < nl - 1)
-    def _():
-        level_copy(1).wait_recv()
-        level_copy(0).wait_send()
-
-    loop(edges, 0, tiles)
+    finish(0)
+    finish(tiles - 1)
     for copy in copies:
         copy.wait_send()
     loop(lambda j: out_copy(j).wait(), 0, tiles)
@@ -344,20 +377,28 @@
     rows = fields * levels
     targets = land_mask.shape[0]
     f32, bf16 = jnp.float32, jnp.bfloat16
-    vmem = pl.BlockSpec(memory_space=pltpu.VMEM)
     land = land_mask.reshape(1, targets)
     result = pl.pallas_call(
         functools.partial(kernel, fields, levels),
         out_shape=jax.ShapeDtypeStruct((rows, targets), f32),
-        in_specs=[pl.BlockSpec(memory_space=pltpu.SMEM)] + [vmem] * 7,
+        in_specs=[pl.BlockSpec(memory_space=pltpu.HBM)] * 8,
         out_specs=pl.BlockSpec(memory_space=pl.ANY),
         scratch_shapes=[
+            pltpu.SMEM(send_slots.shape, jnp.int32),
+            pltpu.VMEM((rows, columns), bf16),
+            pltpu.VMEM((K, targets), jnp.int32),
+            pltpu.VMEM((K, targets), f32),
+            pltpu.VMEM((1, targets), jnp.int32),
+            pltpu.VMEM((NN, targets), jnp.int32),
+            pltpu.VMEM((1, targets), jnp.int32),
+            pltpu.VMEM((fields, levels), f32),
+            pltpu.SemaphoreType.DMA((8,)),
             pltpu.VMEM((columns // B, rows, B), bf16),
             pltpu.VMEM((OFFS, rows, SET), bf16),
-            pltpu.VMEM((OFFS - 1, rows, SET), bf16),
-        ]
-        + [pltpu.VMEM((SET, targets), bf16) for _ in range(OFFS)]
-        + [
+            pltpu.VMEM((2, rows, 2 * SET), bf16),
+            pltpu.VMEM((SET, targets), bf16),
+            pltpu.VMEM((2 * SET, targets), bf16),
+            pltpu.VMEM((2 * SET, targets), bf16),
             pltpu.VMEM((2 * TILE, targets), bf16),
             pltpu.VMEM((K, targets), f32),
             pltpu.VMEM((rows, targets), f32),
@@ -375,7 +416,7 @@
             pltpu.SemaphoreType.DMA((targets // TILE,)),
         ],
         compiler_params=pltpu.CompilerParams(
-            collective_id=0, has_side_effects=True, vmem_limit_bytes=48 * 1024 * 1024
+            collective_id=0, has_side_effects=True, vmem_limit_bytes=64 * 1024 * 1024
         ),
     )(
         send_slots,

time: 60.4 us -> 50.1 us (0.83)
  the two profiles are of different devices: /device:TPU:0 before, /device:TPU:1 now
where the time goes in v2:
time: 50.1 us; the launch traced here: 49.9 us
  Pallas kernels  43 us (86%)
  other arithmetic  5.52 us (11%)
  local copies, waits for them, and re-layouts  1.35 us (3%)
    pallas_call x1, Pallas kernels, on_device(): pl.pallas_call(functools.partial(kernel, fields, levels), out_shape=jax.S...  43 us
    mul x1, other arithmetic, on_device(): updated = land.astype(f32) * result  4.8 us
    unnamed x1, local copies, waits for them, and re-layouts  1.35 us

profile of v2, /device:TPU:1, one launch (start us, length us, event | category | flops | bytes accessed | tf_op | source)
XLA Modules:
  0.0 49.9 jit_solution(13746946618054036696)
XLA Ops:
  0.0 1.4 %copy.9.slots_hbm = s32[1,5,4]{2,1,0:T(8,128)} copy(s32[1,5,4]{1,2,0:T(4,128)} %param.9) | data formatting | bytes 160 | tf_op args[1]
  1.4 43.0 %shard_map.82 = f32[256,4096]{1,0:T(8,128)} custom-call(s32[1,5,4]{2,1,0:T(8,128)} %copy.9.slots_hbm, bf16[256,2048]{1,0:T(8,128)(2,1)} %bitcast.4, s32[8,4096]{1,0:T(8,128)} %col_hbm.1, f32[8,4096]{1,0:T(8,128)} %wt_hbm.1, s32[1,4096]{1,0:T(1,128)} %bitcast.6, s32[6,4096]{1,0:T(8,128)} %near_hbm.1, s32[1,4096]{1,0:T(1,128)} %bitcast.5, f32[8,32]{1,0:T(8,128)} %diff_hbm.1), custom_call_target="tpu_custom_call" | custom-call | tf_op jit(solution)/shard_map/pallas_call | solution.py:381
  44.4 0.7 %convert_element_type.4 = f32[4096]{0:T(1024)S(1)} convert(s32[4096]{0:T(1024)} %param.14) | non-fusion elementwise | flops 4096 | bytes 32768 | tf_op jit(solution)/shard_map/convert_element_type | solution.py:431
  45.1 4.8 %broadcast_multiply_fusion = f32[256,4096]{1,0:T(8,128)} fusion(f32[256,4096]{1,0:T(8,128)} %shard_map.82, f32[4096]{0:T(1024)S(1)} %convert_element_type.4), kind=kLoop, calls=%fused_computation | loop fusion | flops 1048576 | bytes 8404992 | tf_op jit(solution)/shard_map/mul | solution.py:431

commit v3 on v2

--- a/solution.py
+++ b/solution.py
@@ -52,6 +52,7 @@
     wref,
     share_ref,
     rref,
+    qref,
     xm,
     tri_ref,
     dref,
@@ -275,7 +276,7 @@
         )
         copy.start()
         halos.append(copy)
-    loop(last, 1, tiles - 1, 2)
+    loop(last, 1, tiles - 1, 7)
 
     def level_copy(side):
         return pltpu.make_async_remote_copy(
@@ -311,7 +312,8 @@
         beside = jnp.dot(tri_ref[...], value.astype(bf16), preferred_element_type=f32)
         d = dref[...]
         total = gathered[rows : rows + 1]
-        rref[:, tile_of(j)] = (
+        ocean = land_ref[:, tile_of(j)].astype(f32)
+        rref[:, tile_of(j)] = ocean * (
             value * ((1.0 - 2.0 * vertical_rate) - d * total)
             + d * gathered[:rows]
             + vertical_rate * beside
@@ -319,7 +321,7 @@
 
     def out_copy(j):
         return pltpu.make_async_copy(
-            rref.at[:, tile_of(j)], out_ref.at[:, tile_of(j)], out_sem.at[j]
+            qref.at[:, tile_of(j)], out_ref.at[:, tile_of(j)], out_sem.at[j]
         )
 
     def edges(j):
@@ -330,11 +332,14 @@
                     row = f * levels + level
                     at_part = p * fields + f
                     edge = part[at_part : at_part + 1]
-                    rref[row : row + 1, tile_of(j, p * B, B)] += vertical_rate * edge
+                    lanes = tile_of(j, p * B, B)
+                    ocean = vertical_rate * land_ref[:, lanes].astype(f32)
+                    rref[row : row + 1, lanes] += ocean * edge
+        qref[:, tile_of(j)] = rref[:, tile_of(j)].astype(bf16)
         out_copy(j).start()
 
     middle = tiles // 2 - 1
-    loop(final, 1, middle, 2)
+    loop(final, 1, middle, 3)
 
     @pl.when(lev > 0)
     def _():
@@ -351,7 +356,7 @@
         edges(j)
 
     loop(edges, 1, middle)
-    loop(finish, middle, tiles - 1, 2)
+    loop(finish, middle, tiles - 1, 4)
     for copy in halos:
         copy.wait_recv()
     for copy in halos:
@@ -380,7 +385,7 @@
     land = land_mask.reshape(1, targets)
     result = pl.pallas_call(
         functools.partial(kernel, fields, levels),
-        out_shape=jax.ShapeDtypeStruct((rows, targets), f32),
+        out_shape=jax.ShapeDtypeStruct((rows, targets), bf16),
         in_specs=[pl.BlockSpec(memory_space=pltpu.HBM)] * 8,
         out_specs=pl.BlockSpec(memory_space=pl.ANY),
         scratch_shapes=[
@@ -402,6 +407,7 @@
             pltpu.VMEM((2 * TILE, targets), bf16),
             pltpu.VMEM((K, targets), f32),
             pltpu.VMEM((rows, targets), f32),
+            pltpu.VMEM((rows, targets), bf16),
             pltpu.VMEM((rows + 16, targets + 2 * H), bf16),
             pltpu.VMEM((rows, rows), bf16),
             pltpu.VMEM((rows, TILE), f32),
@@ -428,8 +434,7 @@
         land,
         diffusivity,
     )
-    updated = land.astype(f32) * result
-    return updated.reshape(fields, levels, targets)
+    return result.astype(f32).reshape(fields, levels, targets)
 
 
 def solution(mesh):

time: 50.1 us -> 47.7 us (0.952)
  other arithmetic: 5.52 us -> 4.1 us
  Pallas kernels: 43 us -> 42.1 us
    mul x1 -> x0, other arithmetic: 4.8 us -> none  [on_device(): updated = land.astype(f32) * result]
    reshape x0 -> x1, other arithmetic: none -> 4.1 us  [on_device(): return result.astype(f32).reshape(fields, levels, targets)]
    pallas_call x1, Pallas kernels: 43 us -> 42.1 us  [on_device(): pl.pallas_call(functools.partial(kernel, fields, levels), out_shape=jax.S...]
    convert_element_type x1 -> x0, other arithmetic: 0.72 us -> none  [on_device(): updated = land.astype(f32) * result]
where the time goes in v3:
time: 47.7 us; the launch traced here: 47.5 us
  Pallas kernels  42.1 us (88%)
  other arithmetic  4.1 us (9%)
  local copies, waits for them, and re-layouts  1.35 us (3%)
    pallas_call x1, Pallas kernels, on_device(): pl.pallas_call(functools.partial(kernel, fields, levels), out_shape=jax.S...  42.1 us
    reshape x1, other arithmetic, on_device(): return result.astype(f32).reshape(fields, levels, targets)  4.1 us
    unnamed x1, local copies, waits for them, and re-layouts  1.35 us

profile of v3, /device:TPU:1, one launch (start us, length us, event | category | flops | bytes accessed | tf_op | source)
XLA Modules:
  0.0 47.5 jit_solution(13755695072698882348)
XLA Ops:
  0.0 1.4 %copy.9.slots_hbm = s32[1,5,4]{2,1,0:T(8,128)} copy(s32[1,5,4]{1,2,0:T(4,128)} %param.9) | data formatting | bytes 160 | tf_op args[1]
  1.4 42.1 %shard_map.82 = bf16[256,4096]{1,0:T(8,128)(2,1)} custom-call(s32[1,5,4]{2,1,0:T(8,128)} %copy.9.slots_hbm, bf16[256,2048]{1,0:T(8,128)(2,1)} %bitcast.6, s32[8,4096]{1,0:T(8,128)} %col_hbm.1, f32[8,4096]{1,0:T(8,128)} %wt_hbm.1, s32[1,4096]{1,0:T(1,128)} %bitcast.7, s32[6,4096]{1,0:T(8,128)} %near_hbm.1, s32[1,4096]{1,0:T(1,128)} %bitcast.8, f32[8,32]{1,0:T(8,128)} %diff_hbm.1), custom_call_target="tpu_custom_call" | custom-call | tf_op jit(solution)/shard_map/pallas_call | solution.py:386
  43.4 4.1 %convert.1 = f32[8,32,4096]{2,1,0:T(8,128)} convert(bf16[8,32,4096]{2,1,0:T(8,128)(2,1)} %bitcast.5) | non-fusion elementwise | flops 1048576 | bytes 6291456 | tf_op jit(solution)/shard_map/reshape | solution.py:437
